TPU v7x, 128 devices: a whole 4x4x4 slice. The times are simulated.
128 devices in a mesh: state: 8 (over x_hi, z), walk: 16 (over x_lo, y, core).
Axes of the slice: x: 4 (x_hi: 2, x_lo: 2; x = x_hi * 2 + x_lo), y: 4, z: 4, core: 2. Of those that a mesh axis runs over, the one named last changes fastest.
Arguments:
- feats: float32 [8, 128, 80, 128], P('state', 'walk'), may hold values from -6 to 6
- inverses: float32 [8, 128, 2, 40, 40], P('state', 'walk'), may hold values from -1 to 1
- counts: int32 [8], P('state'), may hold values from 32 to 128, as said below
- w_embed: float32 [8, 128, 512], P('state', 'walk'), may hold values from -0.5 to 0.5
- w_qkv: float32 [8, 1, 512, 1536], P('state', None, 'walk'), may hold values from -0.25 to 0.25
- w_out: float32 [8, 1, 512, 512], P('state', None, 'walk'), may hold values from -0.25 to 0.25
- w_mlp: float32 [8, 1, 512, 512], P('state', None, 'walk'), may hold values from -0.25 to 0.25
- w_orb: float32 [8, 512, 80], P('state', 'walk'), may hold values from -0.25 to 0.25
Outputs:
- own_amp: float32 [8, 128], P('state', 'walk')
- margin: float32 [8, 8], P('state')
- penalty: float32 [], replicated
Inputs may be any that keep to these rules, and one draw needn't show every extreme that they name: `counts`: some state has all 128 walkers live.
All inputs are finite; a program needn't handle non-finite values.
Results may differ from a plain program's by a relative error of at most 0.0002.
Values sent between devices are 32-bit elements; how exact they have to be, the bound alone decides.
No kernel may reach another device: no remote copies, remote signals or barrier semaphores. Data moves between devices by JAX's collectives and lax.ppermute only.
A program may use at most 256 MiB of HBM per device.

v0:
```python
import math

import jax
import jax.numpy as jnp
from jax import lax
from jax.sharding import PartitionSpec as P

HEADS = 8
HEAD_DIM = 64
ELEC = 80
HALF = 40
FEAT = 128


def matmul(left, right):
    return jnp.dot(left, right, precision=lax.Precision.HIGHEST, preferred_element_type=jnp.float32)


def normalize(values):
    centred = values - jnp.mean(values, axis=-1, keepdims=True)
    spread = jnp.mean(centred * centred, axis=-1, keepdims=True)
    return centred * lax.rsqrt(spread + 1e-05)


def mix_heads(qkv):
    walkers = qkv.shape[0] // ELEC
    parts = qkv.reshape(walkers, ELEC, 3, HEADS, HEAD_DIM)
    query = parts[:, :, 0]
    keys = parts[:, :, 1]
    values = parts[:, :, 2]
    scores = jnp.einsum(
        "bqhd,bkhd->bhqk", query, keys, precision=lax.Precision.HIGHEST
    ) / math.sqrt(HEAD_DIM)
    weights = jax.nn.softmax(scores, axis=-1)
    mixed = jnp.einsum("bhqk,bkhd->bqhd", weights, values, precision=lax.Precision.HIGHEST)
    return mixed.reshape(walkers * ELEC, HEADS * HEAD_DIM)


def determinant_part(orbitals, inverse):
    walkers = inverse.shape[0]
    phi = orbitals.reshape(walkers, ELEC, ELEC)
    blocks = jnp.stack([phi[:, :HALF, :HALF], phi[:, HALF:, HALF:]], axis=1)
    product = jnp.einsum("bsij,bsjk->bsik", inverse, blocks, precision=lax.Precision.HIGHEST)
    return jnp.log(jnp.mean(product * product, axis=(1, 2, 3)) + 1e-05)


def log_amplitude(rows, inverse, project):
    hidden = project(rows, "embed", 0)
    qkv = project(normalize(hidden), "qkv", 0)
    hidden = hidden + project(mix_heads(qkv), "out", 0)
    hidden = hidden + jnp.tanh(project(normalize(hidden), "mlp", 0))
    return determinant_part(project(hidden, "orb", 0), inverse)


def direct_products(gathered):
    embed, qkv_all, out_all, mlp_all, orbital = gathered

    def project(values, name, layer):
        if name == "embed":
            return matmul(values, embed[0])
        if name == "qkv":
            return matmul(values, qkv_all[0, layer])
        if name == "out":
            return matmul(values, out_all[0, layer])
        if name == "mlp":
            return matmul(values, mlp_all[0, layer])
        return matmul(values, orbital[0])

    return project


def on_device(feats, inverses, counts, w_embed, w_qkv, w_out, w_mlp, w_orb):
    walk_dev = feats.shape[1]
    states = lax.axis_size("state")
    own_index = lax.axis_index("state")
    gathered = (
        lax.all_gather(w_embed, "walk", axis=1, tiled=True),
        lax.all_gather(w_qkv, "walk", axis=2, tiled=True),
        lax.all_gather(w_out, "walk", axis=2, tiled=True),
        lax.all_gather(w_mlp, "walk", axis=2, tiled=True),
        lax.all_gather(w_orb, "walk", axis=1, tiled=True),
    )
    project = direct_products(gathered)
    block_feats = lax.all_gather(feats, "state", axis=0, tiled=True)
    block_inv = lax.all_gather(inverses, "state", axis=0, tiled=True)
    number = block_feats.shape[0]
    rows = block_feats.reshape(number * walk_dev * ELEC, FEAT)
    amps = log_amplitude(rows, block_inv.reshape(number * walk_dev, 2, HALF, HALF), project)
    table = amps.reshape(number, walk_dev)
    received = lax.all_to_all(table, "state", split_axis=0, concat_axis=0, tiled=True)
    own_row = lax.dynamic_slice_in_dim(received, own_index, 1, 0)
    ratio = jnp.exp(received - own_row)
    first = lax.axis_index("walk") * walk_dev
    valid = (first + jnp.arange(walk_dev, dtype=jnp.int32) < counts[0]).astype(jnp.float32)
    scaled = jnp.sum(ratio * valid[None, :], axis=1) / counts[0].astype(jnp.float32)
    row = lax.psum(scaled, "walk")
    full = lax.all_gather(row[None, :], "state", axis=0, tiled=True)
    index_row = jnp.arange(states, dtype=jnp.int32)
    lower = (index_row[None, :] < index_row[:, None]).astype(jnp.float32)
    penalty = 4.0 * jnp.sum(lower * full * full.T)
    return (own_row, row[None, :], penalty)


def solution(mesh):
    in_specs = (
        P("state", "walk", None, None),
        P("state", "walk", None, None, None),
        P("state"),
        P("state", "walk", None),
        P("state", None, "walk", None),
        P("state", None, "walk", None),
        P("state", None, "walk", None),
        P("state", "walk", None),
    )
    out_specs = (P("state", "walk"), P("state", None), P())
    return jax.shard_map(
        on_device, mesh=mesh, in_specs=in_specs, out_specs=out_specs, check_vma=False
    )
```

profile of v0, /device:TPU:6, one launch (start us, length us, event | category | flops | bytes accessed | tf_op | source)
XLA Modules:
  0.0 470.5 jit_solution(17427590956031568505)
XLA Ops:
  7.2 0.0 all-gather.6.cloned.1.call-start
  7.2 0.7 all-gather.6.cloned.1.call-update
  7.9 0.0 all-gather.8.cloned.1.call-start
  7.9 0.7 all-gather.8.cloned.1.call-update
  8.6 0.0 all-gather.10.cloned.1.call-start
  8.7 0.7 all-gather.10.cloned.1.call-update
  9.4 0.0 all-gather.12.cloned.1.call-start
  9.4 0.5 all-gather.12.cloned.1.call-update
  10.0 20.5 %all_gather.25 = f32[1,128,512]{2,1,0:T(8,128)S(1)} all-gather(f32[1,8,512]{2,1,0:T(8,128)} %param.11), channel_id=1, replica_groups=mesh['state'=8,'walk'=16] {'walk'}, dimensions={1}, use_global_device_ids=true | all-gather | bytes 278528 | tf_op jit(solution)/shard_map/all_gather | solution.py:77
  30.4 18.6 %all_gather.29 = f32[1,512,80]{2,0,1:T(1,128)} all-gather(f32[1,32,80]{2,0,1:T(1,128)} %bitcast.88), channel_id=1, replica_groups=mesh['state'=8,'walk'=16] {'walk'}, dimensions={1}, use_global_device_ids=true | all-gather | bytes 174080 | tf_op jit(solution)/shard_map/all_gather | solution.py:81
  49.0 48.2 %all_gather.30 = f32[8,8,2,40,40]{4,3,2,1,0:T(8,128)} all-gather(f32[1,8,2,40,40]{4,3,2,1,0:T(8,128)} %param.9), channel_id=1, replica_groups=mesh['state'=8,'walk'=16] {'state'}, dimensions={0}, use_global_device_ids=true | all-gather | bytes 921600 | tf_op jit(solution)/shard_map/all_gather | solution.py:85
  97.9 0.0 all-gather.6.cloned.1.call-done
  97.9 10.5 %fusion.28 = (f32[5120]{0:T(1024)S(1)}, f32[5120,512]{1,0:T(8,128)S(1)}) fusion(f32[5120,128]{1,0:T(8,128)} %bitcast.81, f32[1,128,512]{2,1,0:T(8,128)S(1)} %all_gather.25), kind=kOutput, calls=%fused_computation.47 | convolution fusion | flops 4029148160 | bytes 13389824 | tf_op jit(solution)/shard_map/dot_general | solution.py:16
  108.4 3.5 multiply_reduce_fusion.2
  111.9 0.5 copy-done
  112.4 5.3 %subtract_multiply_fusion = f32[5120,512]{1,0:T(8,128)} fusion(f32[5120,512]{1,0:T(8,128)S(1)} %get-tuple-element.8, f32[5120]{0:T(1024)S(1)} %add_rsqrt_fusion.1, f32[5120]{0:T(1024)S(1)} %broadcast_multiply_fusion.1), kind=kLoop, calls=%fused_computation.18 | loop fusion | flops 5242880 | bytes 21012480 | tf_op jit(solution)/shard_map/mul | solution.py:22
  117.7 8.2 %all-gather.8.cloned.1.call-done = f32[1,1,512,1536]{3,2,1,0:T(8,128)} async-done(((f32[1,1,32,1536]{3,2,1,0:T(8,128)}), f32[1,1,512,1536]{3,2,1,0:T(8,128)}) %all-gather.8.cloned.1.call-update) | async-done | bytes 3145744 | tf_op jit(solution)/shard_map/all_gather | solution.py:78
  125.9 2.4 copy.22
  128.3 85.0 %fusion.30 = f32[64,80,3,8,64]{1,4,3,2,0:T(8,128)} fusion(f32[64,80,512,1,1]{2,1,4,3,0:T(8,128)} %bitcast.78, f32[3,8,64,512,1]{3,2,1,0,4:T(8,128)S(1)} %bitcast.83), kind=kOutput, calls=%fused_computation.49 | convolution fusion | flops 48318382080 | bytes 45088768 | tf_op jit(solution)/shard_map/dot_general | solution.py:16
  213.3 41.4 %multiply_reduce_fusion = (f32[64,8,80]{2,1,0:T(8,128)}, f32[64,8,80,80]{2,3,1,0:T(8,128)S(1)}) fusion(f32[64,80,3,8,64]{1,4,3,2,0:T(8,128)} %fusion.30), kind=kOutput, calls=%fused_computation.3 | convolution fusion | flops 2523095040 | bytes 46825472 | tf_op jit(solution)/shard_map/bqhd,bkhd->bhqk/dot_general | solution.py:31
  254.7 7.0 %copy-done.1 = f32[64,8,80,80]{2,3,1,0:T(8,128)} copy-done((f32[64,8,80,80]{2,3,1,0:T(8,128)}, f32[64,8,80,80]{2,3,1,0:T(8,128)S(1)}, u32[]{:S(2)}) %copy-start.1) | copy-done | bytes 13107224
  261.7 9.4 %fusion.2 = f32[64,8,80]{2,1,0:T(8,128)} fusion(f32[64,8,80,80]{2,3,1,0:T(8,128)S(1)} %get-tuple-element.10, f32[64,8,80]{2,1,0:T(8,128)} %get-tuple-element.9), kind=kLoop, calls=%fused_computation.4 | loop fusion | flops 9789440 | bytes 13434880 | tf_op jit(solution)/shard_map/reduce_sum | solution.py:34
  271.1 30.0 %fusion.12 = f32[64,80,8,64]{1,3,2,0:T(8,128)S(1)} fusion(f32[64,8,80,80]{2,3,1,0:T(8,128)} %copy-done.1, f32[64,8,80]{2,1,0:T(8,128)} %fusion.2, f32[64,8,80]{2,1,0:T(8,128)} %get-tuple-element.9, f32[64,80,3,8,64]{1,4,3,2,0:T(8,128)} %fusion.30), kind=kOutput, calls=%fused_computation.19 | convolution fusion | flops 2526412800 | bytes 48758784 | tf_op jit(solution)/shard_map/bhqk,bkhd->bqhd/dot_general | solution.py:35
  301.1 11.7 %copy.24 = f32[64,80,8,64]{1,0,3,2:T(8,128)} copy(f32[64,80,8,64]{1,3,2,0:T(8,128)S(1)} %fusion.12) | data formatting | bytes 20971520 | tf_op jit(solution)/shard_map/bhqk,bkhd->bqhd/transpose | solution.py:35
  312.9 17.5 %reshape.80 = f32[5120,512]{0,1:T(8,128)} reshape(f32[64,80,8,64]{1,0,3,2:T(8,128)} %copy.24) | data formatting | bytes 20971520 | tf_op jit(solution)/shard_map/reshape | solution.py:36
  330.4 21.3 %fusion.29 = (f32[5120]{0:T(1024)S(1)}, f32[5120,512]{1,0:T(8,128)S(1)}) fusion(f32[5120,512]{1,0:T(8,128)} %copy-done, f32[5120,512]{0,1:T(8,128)} %reshape.80, f32[1,1,512,512]{3,2,1,0:T(8,128)} %all-gather.10.cloned.1.call-done), kind=kOutput, calls=%fused_computation.48 | convolution fusion | flops 16111365120 | bytes 32526336 | tf_op jit(solution)/shard_map/dot_general | solution.py:16
  351.7 0.0 copy-start.2
  351.7 4.0 copy-done.2
  355.7 3.4 multiply_reduce_fusion.1
  359.2 0.0 copy-start.4
  359.2 0.0 all-gather.12.cloned.1.call-done
  359.2 25.0 %tanh_add_fusion = f32[5120,512]{1,0:T(8,128)S(1)} fusion(f32[5120,512]{1,0:T(8,128)} %copy-done.2, f32[5120]{0:T(1024)S(1)} %add_rsqrt_fusion, f32[5120]{0:T(1024)S(1)} %broadcast_multiply_fusion, f32[1,1,512,512]{3,2,1,0:T(8,128)} %all-gather.12.cloned.1.call-done), kind=kOutput, calls=%fused_computation.9 | convolution fusion | flops 16113991680 | bytes 22061056 | tf_op jit(solution)/shard_map/dot_general | solution.py:16
  384.2 0.0 copy-start.3
  384.2 0.0 copy-done.4
  384.2 8.4 %fusion.31 = f32[64,80,80]{2,1,0:T(8,128)S(1)} fusion(f32[64,80,512]{2,1,0:T(8,128)S(1)} %bitcast.79, f32[512,80,1]{1,0,2:T(8,128)S(1)} %bitcast.84), kind=kOutput, calls=%fused_computation.50 | convolution fusion | flops 2516582400 | bytes 12288000 | tf_op jit(solution)/shard_map/dot_general | solution.py:16
  392.6 0.4 slice_bitcast_fusion.9
  393.0 0.0 copy-done.3
  393.0 5.4 %multiply_reduce_fusion.3 = f32[64]{0:T(128)S(1)} fusion(f32[64,2,40,40]{3,2,1,0:T(8,128)S(1)} %bitcast.80, f32[64,1,40,40]{3,2,0,1:T(8,128)S(1)} %get-tuple-element.4, f32[64,1,40,40]{3,2,0,1:T(8,128)S(1)} %get-tuple-element.3), kind=kOutput, calls=%fused_computation.26 | convolution fusion | flops 98918336 | bytes 1638656 | tf_op jit(solution)/shard_map/bsij,bsjk->bsik/dot_general | solution.py:43
  398.4 0.7 log.15
  399.1 7.4 %all-to-all-start = ((f32[8,1,8]{2,1,0:T(1,128)}), f32[8,1,8]{2,1,0:T(1,128)S(1)}, u32[]{:S(2)}, u32[]{:S(2)}) async-start(f32[8,1,8]{2,1,0:T(1,128)} %bitcast.22), calls=%async_computation | async-start | bytes 8192 | tf_op jit(solution)/shard_map/all_to_all | solution.py:90
  406.5 4.7 all-to-all-done
  411.2 0.5 fusion.25
  411.7 0.1 multiply_reduce_fusion.5
  411.8 27.3 %psum.7 = f32[1,8]{1,0:T(1,128)S(1)} all-reduce(f32[1,8]{1,0:T(1,128)S(1)} %divide_bitcast_fusion), channel_id=1, replica_groups=mesh['state'=8,'walk'=16] {'walk'}, use_global_device_ids=true, to_apply=%region_8.0 | all-reduce | flops 8 | bytes 64 | tf_op jit(solution)/shard_map/psum | solution.py:96
  439.1 22.2 %all-gather = f32[8,1,8]{2,1,0:T(1,128)S(1)} all-gather(f32[1,1,8]{2,1,0:T(1,128)S(1)} %bitcast.89), channel_id=1, replica_groups=mesh['state'=8,'walk'=16] {'state'}, dimensions={0}, use_global_device_ids=true | all-gather | bytes 288 | tf_op jit(solution)/shard_map/all_gather | solution.py:97
  461.3 0.1 copy.29
  461.4 0.6 multiply_reduce_fusion.4
  462.6 0.0 copy-done.5
  (11 shorter events, 0.1 us)
Async XLA Ops:
  7.2 90.7 %all-gather.6.cloned.1.call-start = ((), (), s32[]{:S(2)}) async-start(), calls=%async_computation.1 | async-start | bytes 2949120 | tf_op jit(solution)/shard_map/all_gather | solution.py:84
  7.9 118.0 %all-gather.8.cloned.1.call-start = ((), (), s32[]{:S(2)}) async-start(), calls=%async_computation.2 | async-start | bytes 3342336 | tf_op jit(solution)/shard_map/all_gather | solution.py:78
  8.6 321.8 %all-gather.10.cloned.1.call-start = ((), (), s32[]{:S(2)}) async-start(), calls=%async_computation.3 | async-start | bytes 1114112 | tf_op jit(solution)/shard_map/all_gather | solution.py:79
  9.4 349.8 %all-gather.12.cloned.1.call-start = ((), (), s32[]{:S(2)}) async-start(), calls=%async_computation.4 | async-start | bytes 1114112 | tf_op jit(solution)/shard_map/all_gather | solution.py:80
  108.4 4.0 copy-start
  254.7 7.0 %copy-start.1 = (f32[64,8,80,80]{2,3,1,0:T(8,128)}, f32[64,8,80,80]{2,3,1,0:T(8,128)S(1)}, u32[]{:S(2)}) copy-start(f32[64,8,80,80]{2,3,1,0:T(8,128)S(1)} %get-tuple-element.10) | copy-start | bytes 39321604
  351.7 4.0 copy-start.2
  359.2 25.1 %copy-start.4 = (f32[1,512,80]{2,0,1:T(1,128)S(1)}, f32[1,512,80]{2,0,1:T(1,128)}, u32[]{:S(2)}) copy-start(f32[1,512,80]{2,0,1:T(1,128)} %all_gather.29) | copy-start | bytes 491524
  384.2 8.8 %copy-start.3 = (f32[8,8,2,40,40]{4,3,2,1,0:T(8,128)S(1)}, f32[8,8,2,40,40]{4,3,2,1,0:T(8,128)}, u32[]{:S(2)}) copy-start(f32[8,8,2,40,40]{4,3,2,1,0:T(8,128)} %all_gather.30) | copy-start | bytes 2457604
  399.1 12.1 %all-to-all-start = ((f32[8,1,8]{2,1,0:T(1,128)}), f32[8,1,8]{2,1,0:T(1,128)S(1)}, u32[]{:S(2)}, u32[]{:S(2)}) async-start(f32[8,1,8]{2,1,0:T(1,128)} %bitcast.22), calls=%async_computation | async-start | bytes 8192 | tf_op jit(solution)/shard_map/all_to_all | solution.py:90
  439.1 23.5 %copy-start.5 = (f32[1,8]{1,0:T(1,128)}, f32[1,8]{1,0:T(1,128)S(1)}, u32[]{:S(2)}) copy-start(f32[1,8]{1,0:T(1,128)S(1)} %psum.7) | copy-start | bytes 100
Sparse Core Ops, SparseCore 0:
  10.3 75.4 all-gather.5
  87.5 38.3 all-gather.7
  127.6 32.3 all-gather.9
  161.6 32.4 all-gather.11
where the time goes:
time: 480 us; the launch traced here: 470 us
  matrix products  227 us (47%)
  blocking collectives  137 us (29%)
  local copies, waits for them, and re-layouts  44.8 us (9%)
  other arithmetic  22.4 us (5%)
  between operations  16.6 us (3%)
  waiting for transfers between devices  15.5 us (3%)
  starting transfers between devices  7.53 us (2%)
    dot_general x5, matrix products, matmul(): jnp.dot(left, right, precision=lax.Precision.HIGHEST, preferred_element_t...  150 us
    all_gather x1, blocking collectives, on_device(): block_inv = lax.all_gather(inverses, 'state', axis=0, tiled=True)  48.2 us
    dot_general x1, matrix products, mix_heads(): jnp.einsum('bqhd,bkhd->bhqk', query, keys, precision=lax.Precision.HIGHEST)  41.4 us
    dot_general x1, matrix products, mix_heads(): jnp.einsum('bhqk,bkhd->bqhd', weights, values, precision=lax.Precision.HI...  30 us
    psum x1, blocking collectives, on_device(): row = lax.psum(scaled, 'walk')  27.3 us
    all_gather x1, blocking collectives, on_device(): full = lax.all_gather(row[None, :], 'state', axis=0, tiled=True)  22.2 us
    all_gather x1, blocking collectives, on_device(): lax.all_gather(w_embed, 'walk', axis=1, tiled=True)  20.5 us
    all_gather x1, blocking collectives, on_device(): lax.all_gather(w_orb, 'walk', axis=1, tiled=True)  18.6 us
  transfers between devices with their start and end apart: 5, of which 2 were waited for; matrix products, arithmetic and copies ran while one was open for 51% of the time, Pallas kernels for 0%

commit v1 on v0

v1 whole, which is shorter than its diff:
```python
import math

import jax
import jax.numpy as jnp
from jax import lax
from jax.experimental import pallas as pl
from jax.experimental.pallas import tpu as pltpu
from jax.sharding import PartitionSpec as P

ELEC = 80
HALF = 40
BF = jnp.bfloat16
F32 = jnp.float32
OUT_AT, MLP_AT, ORB_AT, EMB_AT, PACKED = 1536, 2048, 2560, 2688, 2816
SAFE = 90.0


def dot(left, right):
    return jnp.dot(left, right, preferred_element_type=F32)


def dot_nt(left, right):
    return lax.dot_general(
        left, right, (((1,), (1,)), ((), ())), preferred_element_type=F32
    )


def split(values):
    high = values.astype(BF)
    return high, (values - high.astype(F32)).astype(BF)


def dot3(left, right, product):
    left_high, left_low = split(left)
    right_high, right_low = split(right)
    return (
        product(left_high, right_high)
        + product(left_low, right_high)
        + product(left_high, right_low)
    )


def weight_dot(values, ref, precise):
    if precise:
        high, low = split(values)
        return dot(high, ref[0]) + dot(low, ref[0]) + dot(high, ref[1])
    return dot(values.astype(BF), ref[0])


def prepare(packed, w_in, w_back, w_mlp, w_orb):
    shards = packed.shape[0] // 32
    parts = []
    for j in range(4):
        rows = [packed[i * 32 + 8 * j : i * 32 + 8 * j + 8, EMB_AT:PACKED] for i in range(shards)]
        parts.append(jnp.concatenate(rows, axis=0))
    embed = jnp.concatenate(parts, axis=1)
    centred = embed - jnp.mean(embed, axis=1, keepdims=True)

    def put(at, values):
        high, low = split(values)
        columns = slice(at, at + values.shape[1])
        w_in[0, 0:128, columns] = high
        w_in[0, 128:256, columns] = high
        w_in[1, 0:128, columns] = low

    put(0, embed)
    query = dot3(centred, packed[:, 0:512], dot) * (math.log2(math.e) / 8.0)
    keys = dot3(centred, packed[:, 512:1024], dot)
    values = dot3(centred, packed[:, 1024:1536], dot)
    lane = lax.broadcasted_iota(jnp.int32, (128, 128), 1)
    for head in range(8):
        pair = slice(128 * (head // 2), 128 * (head // 2) + 128)
        keep = (lane < 64) if head % 2 == 0 else (lane >= 64)
        put(512 + 128 * head, dot3(jnp.where(keep, query[:, pair], 0.0), keys[:, pair], dot_nt))
        back = dot3(jnp.where(keep, values[:, pair], 0.0), packed[pair, OUT_AT:MLP_AT], dot)
        high, low = split(back)
        w_back[0, 128 * head : 128 * head + 128, :] = high
        w_back[1, 128 * head : 128 * head + 128, :] = low
    for ref, at, width in ((w_mlp, MLP_AT, 512), (w_orb, ORB_AT, 128)):
        high, low = split(packed[:, at : at + width])
        ref[0] = high
        ref[1] = low


def centre(values):
    centred = values - jnp.mean(values, axis=1, keepdims=True)
    spread = jnp.mean(centred * centred, axis=1, keepdims=True)
    return centred, lax.rsqrt(spread + 1e-05)


def walkers_block(feats, inverse, number, w_in, w_back, w_mlp, w_orb, scores, precise):
    feats_high, feats_low = split(feats)
    hidden = dot(jnp.concatenate([feats_high, feats_low], axis=1), w_in[0, :, 0:512])
    if precise:
        hidden = hidden + dot(feats_high, w_in[1, 0:128, 0:512])
    _, scale = centre(hidden)
    high, low = split(feats * scale)
    query = dot(jnp.concatenate([high, low], axis=1), w_in[0, :, 512:1536])
    if precise:
        query = query + dot(high, w_in[1, 0:128, 512:1536])
    empty = jnp.zeros((128 - ELEC, 128), BF)

    def padded(values, w):
        return jnp.concatenate([values[ELEC * w : ELEC * w + ELEC], empty], axis=0)

    largest = jnp.zeros((8, 128), F32)
    for w in range(number):
        rows = query[ELEC * w : ELEC * w + ELEC]
        stacked = jnp.concatenate([rows[:, 128 * h : 128 * h + 128] for h in range(8)], axis=0)
        if precise:
            stacked_high, stacked_low = split(stacked)
            score = (
                dot_nt(stacked_high, padded(high, w))
                + dot_nt(stacked_low, padded(high, w))
                + dot_nt(stacked_high, padded(low, w))
            )
        else:
            score = dot_nt(stacked.astype(BF), padded(high, w))
        scores[w] = score
        sizes = jnp.abs(score).reshape(8 * ELEC // 8, 8, 128)
        largest = jnp.maximum(largest, jnp.max(sizes, axis=0))

    @pl.when(jnp.logical_not(jnp.max(largest) < SAFE))
    def _():
        lane = lax.broadcasted_iota(jnp.int32, (8 * ELEC, 128), 1)

        @pl.loop(0, number)
        def _(w):
            score = scores[w]
            top = jnp.max(jnp.where(lane < ELEC, score, -jnp.inf), axis=1, keepdims=True)
            scores[w] = jnp.where(lane < ELEC, score - top, 0.0)

    row = lax.broadcasted_iota(jnp.int32, (128, 128), 0)
    live = jnp.where(row < ELEC, 1.0, 0.0).astype(BF)
    mixed = []
    for w in range(number):
        weights = jnp.exp2(scores[w])
        right = jnp.concatenate([padded(high, w), live], axis=1)
        if precise:
            weights_high, weights_low = split(weights)
            both = dot(weights_high, right) + dot(weights_low, right)
            own = (both[:, :128] + dot(weights_high, padded(low, w))) / both[:, 128:]
        else:
            both = dot(weights.astype(BF), right)
            own = (both[:, :128] / both[:, 128:]).astype(BF)
        mixed.append(
            jnp.concatenate([own[ELEC * h : ELEC * h + ELEC] for h in range(8)], axis=1)
        )
    hidden = hidden + weight_dot(jnp.concatenate(mixed, axis=0), w_back, precise)
    centred, scale = centre(hidden)
    hidden = hidden + jnp.tanh(weight_dot(centred * scale, w_mlp, precise))
    orbitals = weight_dot(hidden, w_orb, precise)
    lane = lax.broadcasted_iota(jnp.int32, (HALF, 128), 1)
    results = []
    for w in range(number):
        total = jnp.zeros((HALF, 128), F32)
        for spin in range(2):
            first = HALF * spin
            product = jnp.dot(
                inverse[w][first : first + HALF, :HALF],
                orbitals[ELEC * w + first : ELEC * w + first + HALF],
                precision=lax.Precision.HIGHEST,
                preferred_element_type=F32,
            )
            product = jnp.where((lane >= first) & (lane < first + HALF), product, 0.0)
            total = total + product * product
        total = jnp.sum(jnp.sum(total, axis=0, keepdims=True), axis=1, keepdims=True)
        results.append(jnp.log(total / (2.0 * HALF * HALF) + 1e-05))
    return results


def network_kernel(
    place, counts, local, group, other, packed, table, own, w_in, w_back, w_mlp, w_orb, scores
):
    step = pl.program_id(0)
    number = 8
    state = place[step]
    lane = lax.broadcasted_iota(jnp.int32, (1, 128), 1)

    def unpacked(pack):
        found = []
        for w in range(number):
            third = w % 3
            part = pack[w // 3]
            found.append(part if third == 0 else pltpu.roll(part, 128 - HALF * third, 1))
        return found

    @pl.when(step == 0)
    def _():
        prepare(packed, w_in, w_back, w_mlp, w_orb)
        feats = local[0:number].reshape(number * ELEC, 128)
        results = walkers_block(
            feats, unpacked(local[number:]), number, w_in, w_back, w_mlp, w_orb, scores, True
        )
        row = jnp.where(lane == 64, counts[0].astype(F32), 0.0)
        alone = jnp.zeros((1, 128), F32)
        for w in range(number):
            row = row + jnp.where(lane == state * 8 + w, results[w], 0.0)
            alone = alone + jnp.where(lane == w, results[w], 0.0)
        own[...] = alone
        table[...] = jnp.broadcast_to(row, table.shape)

    @pl.when(step > 0)
    def _():
        near = step < 4
        block = jnp.where(near, group[0], other[0])
        feats = block[0:number].reshape(number * ELEC, 128)
        results = walkers_block(
            feats, unpacked(block[number:]), number, w_in, w_back, w_mlp, w_orb, scores, False
        )
        row = jnp.zeros((1, 128), F32)
        for w in range(number):
            row = row + jnp.where(lane == state * 8 + w, results[w], 0.0)
        table[...] += jnp.broadcast_to(row, table.shape)


def networks(place, counts, local, group, other, packed):
    return pl.pallas_call(
        network_kernel,
        grid_spec=pltpu.PrefetchScalarGridSpec(
            num_scalar_prefetch=2,
            grid=(8,),
            in_specs=[
                pl.BlockSpec((11, ELEC, 128), lambda i, place, counts: (0, 0, 0)),
                pl.BlockSpec(
                    (1, 11, ELEC, 128),
                    lambda i, place, counts: (place[jnp.clip(i, 1, 3)] % 4, 0, 0, 0),
                ),
                pl.BlockSpec(
                    (1, 11, ELEC, 128),
                    lambda i, place, counts: (place[jnp.maximum(i, 4)] % 4, 0, 0, 0),
                ),
                pl.BlockSpec((512, PACKED), lambda i, place, counts: (0, 0)),
            ],
            out_specs=[
                pl.BlockSpec((128, 128), lambda i, place, counts: (0, 0)),
                pl.BlockSpec((1, 128), lambda i, place, counts: (0, 0)),
            ],
            scratch_shapes=[
                pltpu.VMEM((2, 256, 1536), BF),
                pltpu.VMEM((2, 1024, 512), BF),
                pltpu.VMEM((2, 512, 512), BF),
                pltpu.VMEM((2, 512, 128), BF),
                pltpu.VMEM((8, 8 * ELEC, 128), F32),
            ],
        ),
        out_shape=[
            jax.ShapeDtypeStruct((128, 128), F32),
            jax.ShapeDtypeStruct((1, 128), F32),
        ],
        compiler_params=pltpu.CompilerParams(vmem_limit_bytes=56 * 2**20),
        cost_estimate=pl.CostEstimate(
            flops=30_000_000_000, bytes_accessed=10_000_000, transcendentals=8_000_000
        ),
    )(place, counts, local, group, other, packed)


def margin_kernel(place, received, margin, penalty):
    table = received[...]
    lane = lax.broadcasted_iota(jnp.int32, (16, 128), 1)
    block = lax.broadcasted_iota(jnp.int32, (16, 128), 0)
    owner = lane // 8
    own = jnp.zeros((16, 128), F32)
    counts = jnp.ones((1, 128), F32)
    for s in range(8):
        own = jnp.where(owner == s, table[16 * s : 16 * s + 16], own)
        counts = jnp.where(owner[0:1] == s, table[16 * s : 16 * s + 1, 64:65], counts)
    walker = (block * 8 + lane % 8).astype(F32)
    valid = (walker < counts) & (lane < 64)
    rows = []
    for t in range(8):
        ratio = jnp.exp(jnp.where(valid, table[16 * t : 16 * t + 16] - own, -jnp.inf))
        rows.append(jnp.sum(ratio, axis=0, keepdims=True))
    sums = jnp.concatenate(rows, axis=0) / counts
    pick = (
        lax.broadcasted_iota(jnp.int32, (8, 128), 1) // 8
        == lax.broadcasted_iota(jnp.int32, (8, 128), 0)
    ).astype(F32)

    def exact(left, right):
        return lax.dot_general(
            left,
            right,
            (((1,), (1,)), ((), ())),
            precision=lax.Precision.HIGHEST,
            preferred_element_type=F32,
        )

    by_state = exact(pick, sums)
    by_network = exact(sums, pick)
    row = lax.broadcasted_iota(jnp.int32, (8, 8), 0)
    column = lax.broadcasted_iota(jnp.int32, (8, 8), 1)
    margin[...] = jnp.sum(jnp.where(row == place[0], by_state, 0.0), axis=0, keepdims=True)
    product = jnp.where(column < row, by_state * by_network, 0.0)
    total = jnp.sum(jnp.sum(product, axis=0, keepdims=True), axis=1, keepdims=True)
    penalty[...] = 4.0 * total


def margins(place, received):
    return pl.pallas_call(
        margin_kernel,
        grid_spec=pltpu.PrefetchScalarGridSpec(
            num_scalar_prefetch=1,
            grid=(1,),
            in_specs=[pl.BlockSpec((128, 128), lambda i, place: (0, 0))],
            out_specs=[
                pl.BlockSpec((1, 8), lambda i, place: (0, 0)),
                pl.BlockSpec((1, 1), lambda i, place: (0, 0)),
            ],
        ),
        out_shape=[
            jax.ShapeDtypeStruct((1, 8), F32),
            jax.ShapeDtypeStruct((1, 1), F32),
        ],
    )(place, received)


def on_device(feats, inverses, counts, w_embed, w_qkv, w_out, w_mlp, w_orb):
    me = lax.axis_index("state")
    packed = jnp.concatenate(
        [
            w_qkv[0, 0],
            w_out[0, 0],
            w_mlp[0, 0],
            jnp.pad(w_orb[0], ((0, 0), (0, 128 - ELEC))),
            jnp.concatenate([w_embed[0, :, 128 * j : 128 * j + 128] for j in range(4)], axis=0),
        ],
        axis=1,
    )
    packed = lax.all_gather(packed, "walk", axis=0, tiled=True)
    flat = jnp.pad(inverses[0].reshape(8, ELEC, HALF), ((0, 1), (0, 0), (0, 0)))
    flat = flat.reshape(3, 3, ELEC, HALF)
    flat = jnp.concatenate(
        [flat[:, 0], flat[:, 1], flat[:, 2], jnp.zeros((3, ELEC, 8), F32)], axis=2
    )
    local = jnp.concatenate([feats[0], flat], axis=0)
    partner = lax.ppermute(local, "state", [(i, i ^ 4) for i in range(8)])

    def along(block):
        wide = jnp.broadcast_to(block[None], (4,) + block.shape)
        return lax.all_to_all(
            wide, "state", 0, 0, axis_index_groups=[[0, 1, 2, 3], [4, 5, 6, 7]]
        )

    group = along(local)
    other = along(partner)
    high = me // 4
    low = me % 4
    near = [high * 4 + (low + i) % 4 for i in range(4)]
    far = [(1 - high) * 4 + i for i in range(4)]
    place = jnp.stack(near + far).astype(jnp.int32)
    table, own = networks(place, counts, local, group, other, packed)
    received = lax.all_to_all(
        table.reshape(128, 1, 128), ("state", "walk"), 0, 0, tiled=True
    )
    margin, penalty = margins(place, received.reshape(128, 128))
    return own[:, 0:8], margin, penalty[0, 0]


def solution(mesh):
    in_specs = (
        P("state", "walk", None, None),
        P("state", "walk", None, None, None),
        P("state"),
        P("state", "walk", None),
        P("state", None, "walk", None),
        P("state", None, "walk", None),
        P("state", None, "walk", None),
        P("state", "walk", None),
    )
    out_specs = (P("state", "walk"), P("state", None), P())
    return jax.shard_map(
        on_device, mesh=mesh, in_specs=in_specs, out_specs=out_specs, check_vma=False
    )
```

time: 480 us -> 151 us (0.31)
  the two profiles are of different devices: /device:TPU:6 before, /device:TPU:1 now
where the time goes in v1:
time: 151 us
  Pallas kernels  52.5 us (35%)
  waiting for transfers between devices  39.5 us (26%)
  blocking collectives  20.5 us (14%)
  between operations  14.9 us (10%)
  starting transfers between devices  13 us (9%)
  local copies, waits for them, and re-layouts  10.3 us (7%)
    pallas_call x1, Pallas kernels, networks(): pl.pallas_call(network_kernel, grid_spec=pltpu.PrefetchScalarGridSpec(num...  50.1 us
    all_to_all x2, waiting for transfers between devices, along(): lax.all_to_all(wide, 'state', 0, 0, axis_index_groups=[[0, 1, 2, 3], [4,...  21 us
    all_to_all x1, blocking collectives, on_device(): lax.all_to_all(table.reshape(128, 1, 128), ('state', 'walk'), 0, 0, tiled...  20.5 us
    ppermute x1, waiting for transfers between devices, on_device(): partner = lax.ppermute(local, 'state', [(i, i ^ 4) for i in range(8)])  18.5 us
    all_to_all x2, starting transfers between devices, along(): lax.all_to_all(wide, 'state', 0, 0, axis_index_groups=[[0, 1, 2, 3], [4,...  10.3 us
    unnamed x15, local copies, waits for them, and re-layouts  4.84 us
  transfers between devices with their start and end apart: 4, of which 3 were waited for; matrix products, arithmetic and copies ran while one was open for 3% of the time, Pallas kernels for 0%

profile of v1, /device:TPU:1, one launch (start us, length us, event | category | flops | bytes accessed | tf_op | source)
XLA Modules:
  0.0 150.9 jit_solution(15963155923176716134)
XLA Ops:
  7.2 0.0 copy-start.3
  7.2 0.0 all-gather.2.cloned.1.call-start
  7.2 1.0 bitcast_dynamic-update-slice_fusion
  8.2 0.7 slice_bitcast_fusion.3
  8.9 0.8 bitcast_dynamic-update-slice_fusion.2
  9.8 0.8 bitcast_dynamic-update-slice_fusion.1
  10.6 0.7 pad_dynamic-update-slice_fusion
  11.4 0.0 copy-start.2
  11.4 0.7 copy-done.2
  12.1 0.0 all-gather.2.cloned.1.call-update
  12.1 1.1 copy.20
  13.3 0.1 copy.23
  13.4 0.1 copy.22
  13.5 0.1 copy.21
  13.6 0.1 pad.18.clone
  13.7 0.0 copy-done.3
  13.7 0.1 maximum_maximum_fusion.local
  13.8 0.0 copy-start.1
  13.8 1.4 broadcast_in_dim.7
  15.2 5.9 %all-to-all-start = ((f32[4,11,80,128]{3,2,1,0:T(8,128)}), f32[4,11,80,128]{3,2,1,0:T(8,128)S(1)}, u32[]{:S(2)}, u32[]{:S(2)}) async-start(f32[4,11,80,128]{3,2,1,0:T(8,128)} %broadcast_in_dim.7), calls=%async_computation | async-start | bytes 3604480 | tf_op jit(solution)/shard_map/all_to_all | solution.py:341
  21.1 0.0 copy-done.1
  21.1 2.7 %collective-permute-start = (f32[11,80,128]{2,1,0:T(8,128)S(1)}, f32[11,80,128]{2,1,0:T(8,128)S(1)}, u32[]{:S(2)}, u32[]{:S(2)}) collective-permute-start(f32[11,80,128]{2,1,0:T(8,128)S(1)} %maximum_maximum_fusion.local), channel_id=1, source_target_pairs={{0,64},{16,80},{32,96},{48,112},{64,0},{80,16},{96,32},{112,48},{1... | collective-permute-start | bytes 1351688 | tf_op jit(solution)/shard_map/ppermute | solution.py:337
  23.8 18.5 %collective-permute-done = f32[11,80,128]{2,1,0:T(8,128)S(1)} collective-permute-done((f32[11,80,128]{2,1,0:T(8,128)S(1)}, f32[11,80,128]{2,1,0:T(8,128)S(1)}, u32[]{:S(2)}, u32[]{:S(2)}) %collective-permute-start) | collective-permute-done | bytes 450592 | tf_op jit(solution)/shard_map/ppermute | solution.py:337
  42.3 1.0 all-to-all-done.group
  43.3 0.0 copy-start
  43.3 1.4 broadcast_in_dim.8
  44.8 0.4 copy-done
  45.2 4.4 %all-to-all-start.1 = ((f32[4,11,80,128]{3,2,1,0:T(8,128)}), f32[4,11,80,128]{3,2,1,0:T(8,128)}, u32[]{:S(2)}, u32[]{:S(2)}) async-start(f32[4,11,80,128]{3,2,1,0:T(8,128)} %broadcast_in_dim.8), calls=%async_computation.1 | async-start | bytes 3604480 | tf_op jit(solution)/shard_map/all_to_all | solution.py:341
  50.3 0.7 stack.35.place
  51.0 20.0 %all-to-all-done.1.other = f32[4,11,80,128]{3,2,1,0:T(8,128)} async-done(((f32[4,11,80,128]{3,2,1,0:T(8,128)}), f32[4,11,80,128]{3,2,1,0:T(8,128)}, u32[]{:S(2)}, u32[]{:S(2)}) %all-to-all-start.1) | async-done | bytes 1802272 | tf_op jit(solution)/shard_map/all_to_all | solution.py:341
  71.0 0.0 all-gather.2.cloned.1.call-done.packed
  71.0 50.1 %shard_map.103 = (f32[128,128]{1,0:T(8,128)}, f32[1,128]{1,0:T(1,128)}) custom-call(s32[8]{0:T(128)} %stack.35.place, s32[1]{0:T(128)S(6)} %copy.28.counts, f32[11,80,128]{2,1,0:T(8,128)} %copy-done.1, f32[4,11,80,128]{3,2,1,0:T(8,128)} %copy-done, f32[4,11,80,128]{3,2,1,0:T(8,128)} %all-to-all-done.1.other, f32[512,2816]{1,0:T(8,128)} %all-gather.2.cloned.1.call-done.packed), custom_call_target="tpu_custom_call" | custom-call | flops 30000001024 | bytes 10000000 | tf_op jit(solution)/shard_map/pallas_call | solution.py:218
  121.1 20.5 %all_to_all.15 = f32[128,1,128]{2,1,0:T(1,128)} all-to-all(f32[128,1,128]{2,1,0:T(1,128)} %bitcast.42), channel_id=1, replica_groups=mesh['state'=8,'walk'=16] {'state','walk'}, dimensions={0} | all-to-all | bytes 131072 | tf_op jit(solution)/shard_map/all_to_all | solution.py:353
  141.7 2.3 %shard_map.104 = (f32[1,8]{1,0:T(1,128)}, f32[1,1]{1,0:T(1,128)}) custom-call(s32[8]{0:T(128)} %stack.35.place, f32[128,128]{1,0:T(8,128)} %bitcast.41), custom_call_target="tpu_custom_call" | custom-call | tf_op jit(solution)/shard_map/pallas_call | solution.py:300
  (4 shorter events, 0.0 us)
Async XLA Ops:
  7.2 6.5 %copy-start.3 = (f32[1,8,80,128]{3,2,1,0:T(8,128)S(1)}, f32[1,8,80,128]{3,2,1,0:T(8,128)}, u32[]{:S(2)}) copy-start(f32[1,8,80,128]{3,2,1,0:T(8,128)} %param.8) | copy-start | bytes 983044
  7.2 63.8 %all-gather.2.cloned.1.call-start = ((), (), s32[]{:S(2)}) async-start(), calls=%async_computation.3 | async-start | bytes 6127616 | tf_op jit(solution)/shard_map/all_gather | solution.py:330
  11.4 0.7 copy-start.2
  13.8 7.2 %copy-start.1 = (f32[11,80,128]{2,1,0:T(8,128)}, f32[11,80,128]{2,1,0:T(8,128)S(1)}, u32[]{:S(2)}) copy-start(f32[11,80,128]{2,1,0:T(8,128)S(1)} %maximum_maximum_fusion.local) | copy-start | bytes 1351684
  15.2 28.1 %all-to-all-start = ((f32[4,11,80,128]{3,2,1,0:T(8,128)}), f32[4,11,80,128]{3,2,1,0:T(8,128)S(1)}, u32[]{:S(2)}, u32[]{:S(2)}) async-start(f32[4,11,80,128]{3,2,1,0:T(8,128)} %broadcast_in_dim.7), calls=%async_computation | async-start | bytes 3604480 | tf_op jit(solution)/shard_map/all_to_all | solution.py:341
  21.1 21.2 %collective-permute-start = (f32[11,80,128]{2,1,0:T(8,128)S(1)}, f32[11,80,128]{2,1,0:T(8,128)S(1)}, u32[]{:S(2)}, u32[]{:S(2)}) collective-permute-start(f32[11,80,128]{2,1,0:T(8,128)S(1)} %maximum_maximum_fusion.local), channel_id=1, source_target_pairs={{0,64},{16,80},{32,96},{48,112},{64,0},{80,16},{96,32},{112,48},{1... | collective-permute-start | bytes 1351688 | tf_op jit(solution)/shard_map/ppermute | solution.py:337
  43.3 1.8 %copy-start = (f32[4,11,80,128]{3,2,1,0:T(8,128)}, f32[4,11,80,128]{3,2,1,0:T(8,128)S(1)}, u32[]{:S(2)}) copy-start(f32[4,11,80,128]{3,2,1,0:T(8,128)S(1)} %all-to-all-done.group) | copy-start | bytes 5406724
  45.2 25.8 %all-to-all-start.1 = ((f32[4,11,80,128]{3,2,1,0:T(8,128)}), f32[4,11,80,128]{3,2,1,0:T(8,128)}, u32[]{:S(2)}, u32[]{:S(2)}) async-start(f32[4,11,80,128]{3,2,1,0:T(8,128)} %broadcast_in_dim.8), calls=%async_computation.1 | async-start | bytes 3604480 | tf_op jit(solution)/shard_map/all_to_all | solution.py:341
Sparse Core Ops, SparseCore 0:
  12.3 51.9 all-gather.1

commit v2 on v1

v2 whole, which is shorter than its diff:
```python
import math

import jax
import jax.numpy as jnp
from jax import lax
from jax.experimental import pallas as pl
from jax.experimental.pallas import tpu as pltpu
from jax.sharding import PartitionSpec as P

ELEC = 80
HALF = 40
BF = jnp.bfloat16
F32 = jnp.float32
OUT_AT, MLP_AT, ORB_AT, EMB_AT, PACKED = 1536, 2048, 2560, 2688, 2816
SAFE = 90.0


def dot(left, right):
    return jnp.dot(left, right, preferred_element_type=F32)


def dot_nt(left, right):
    return lax.dot_general(
        left, right, (((1,), (1,)), ((), ())), preferred_element_type=F32
    )


def split(values):
    high = values.astype(BF)
    return high, (values - high.astype(F32)).astype(BF)


def dot3(left, right, product):
    left_high, left_low = split(left)
    right_high, right_low = split(right)
    return (
        product(left_high, right_high)
        + product(left_low, right_high)
        + product(left_high, right_low)
    )


def weight_dot(values, ref, precise):
    if precise:
        high, low = split(values)
        return dot(high, ref[0]) + dot(low, ref[0]) + dot(high, ref[1])
    return dot(values.astype(BF), ref[0])


def prepare(packed, w_in, w_back, w_mlp, w_orb, copies):
    shards = packed.shape[0] // 32
    copies[0].wait()
    parts = []
    for j in range(4):
        rows = [packed[i * 32 + 8 * j : i * 32 + 8 * j + 8, EMB_AT:PACKED] for i in range(shards)]
        parts.append(jnp.concatenate(rows, axis=0))
    embed = jnp.concatenate(parts, axis=1)
    centred = embed - jnp.mean(embed, axis=1, keepdims=True)

    def put(at, values):
        high, low = split(values)
        columns = slice(at, at + values.shape[1])
        w_in[0, 0:128, columns] = high
        w_in[0, 128:256, columns] = high
        w_in[1, 0:128, columns] = low

    put(0, embed)
    copies[1].wait()
    query = dot3(centred, packed[:, 0:512], dot) * (math.log2(math.e) / 8.0)
    copies[2].wait()
    keys = dot3(centred, packed[:, 512:1024], dot)
    copies[3].wait()
    values = dot3(centred, packed[:, 1024:1536], dot)
    lane = lax.broadcasted_iota(jnp.int32, (128, 128), 1)
    copies[4].wait()
    for head in range(8):
        pair = slice(128 * (head // 2), 128 * (head // 2) + 128)
        keep = (lane < 64) if head % 2 == 0 else (lane >= 64)
        put(512 + 128 * head, dot3(jnp.where(keep, query[:, pair], 0.0), keys[:, pair], dot_nt))
        back = dot3(jnp.where(keep, values[:, pair], 0.0), packed[pair, OUT_AT:MLP_AT], dot)
        high, low = split(back)
        w_back[0, 128 * head : 128 * head + 128, :] = high
        w_back[1, 128 * head : 128 * head + 128, :] = low
    copies[5].wait()
    for ref, at, width in ((w_mlp, MLP_AT, 512), (w_orb, ORB_AT, 128)):
        high, low = split(packed[:, at : at + width])
        ref[0] = high
        ref[1] = low


def centre(values):
    centred = values - jnp.mean(values, axis=1, keepdims=True)
    spread = jnp.mean(centred * centred, axis=1, keepdims=True)
    return centred, lax.rsqrt(spread + 1e-05)


def walkers_block(feats, inverse, weights, precise, shift, out):
    w_in, w_back, w_mlp, w_orb = weights
    number = feats.shape[0] // ELEC
    feats_high, feats_low = split(feats)
    hidden = dot(jnp.concatenate([feats_high, feats_low], axis=1), w_in[0, :, 0:512])
    if precise:
        hidden = hidden + dot(feats_high, w_in[1, 0:128, 0:512])
    yield
    _, scale = centre(hidden)
    high, low = split(feats * scale)
    yield
    query = dot(jnp.concatenate([high, low], axis=1), w_in[0, :, 512:1536])
    if precise:
        query = query + dot(high, w_in[1, 0:128, 512:1536])
    yield
    empty = jnp.zeros((128 - ELEC, 128), BF)
    nothing = jnp.zeros((128, 128), BF)

    def padded(values, w):
        return jnp.concatenate([values[ELEC * w : ELEC * w + ELEC], empty], axis=0)

    def keys(values, w):
        if number == 1:
            return padded(values, w)
        above = jnp.concatenate([padded(values, w), nothing], axis=1)
        below = jnp.concatenate([nothing, padded(values, w + 1)], axis=1)
        return jnp.concatenate([above, below], axis=0)

    def by_head(w):
        rows = query[ELEC * w : ELEC * w + ELEC]
        return jnp.concatenate([rows[:, 128 * h : 128 * h + 128] for h in range(8)], axis=0)

    scores = []
    for w in range(0, number, 2):
        pair = range(w, min(w + 2, number))
        stacked = jnp.concatenate([by_head(u) for u in pair], axis=1)
        right = keys(high, w)
        if precise:
            stacked_high, stacked_low = split(stacked)
            score = (
                dot_nt(stacked_high, right)
                + dot_nt(stacked_low, right)
                + dot_nt(stacked_high, keys(low, w))
            )
        else:
            score = dot_nt(stacked.astype(BF), right)
        scores += [score[:, 128 * i : 128 * i + 128] for i in range(len(pair))]
    yield
    largest = jnp.zeros((8, 128), F32)
    lane = lax.broadcasted_iota(jnp.int32, (8 * ELEC, 128), 1)
    weights = []
    for score in scores:
        if shift:
            top = jnp.max(jnp.where(lane < ELEC, score, -jnp.inf), axis=1, keepdims=True)
            score = jnp.where(lane < ELEC, score - top, 0.0)
        else:
            sizes = jnp.abs(score).reshape(ELEC, 8, 128)
            largest = jnp.maximum(largest, jnp.max(sizes, axis=0))
        power = jnp.exp2(score)
        weights.append(split(power) if precise else power.astype(BF))
    yield
    row = lax.broadcasted_iota(jnp.int32, (128, 128), 0)
    live = jnp.where(row < ELEC, 1.0, 0.0).astype(BF)
    sums = []
    for w in range(number):
        right = jnp.concatenate([padded(high, w), live], axis=1)
        if precise:
            weights_high, weights_low = weights[w]
            both = dot(weights_high, right) + dot(weights_low, right)
            sums.append((both[:, :128] + dot(weights_high, padded(low, w)), both[:, 128:]))
        else:
            both = dot(weights[w], right)
            sums.append((both[:, :128], both[:, 128:]))
    yield
    mixed = []
    for top, bottom in sums:
        mean = top / bottom
        if not precise:
            mean = mean.astype(BF)
        mixed.append(
            jnp.concatenate([mean[ELEC * h : ELEC * h + ELEC] for h in range(8)], axis=1)
        )
    yield
    hidden = hidden + weight_dot(jnp.concatenate(mixed, axis=0), w_back, precise)
    yield
    centred, scale = centre(hidden)
    normal = centred * scale
    if not precise:
        normal = normal.astype(BF)
    yield
    inner = weight_dot(normal, w_mlp, precise)
    yield
    hidden = hidden + jnp.tanh(inner)
    if not precise:
        hidden = hidden.astype(BF)
    yield
    orbitals = weight_dot(hidden, w_orb, precise)
    yield
    lane = lax.broadcasted_iota(jnp.int32, (HALF, 128), 1)
    totals = []
    for first in range(0, number, 3):
        group = range(first, min(first + 3, number))
        rows = HALF * len(group)
        total = jnp.zeros((rows, 128), F32)
        lanes = lax.broadcasted_iota(jnp.int32, (rows, 128), 1)
        for spin in range(2):
            given = inverse(first // 3, spin)
            left = jnp.concatenate(
                [
                    jnp.where((lane >= HALF * i) & (lane < HALF * i + HALF), given, 0.0)
                    for i in range(len(group))
                ],
                axis=0,
            )
            at = HALF * spin
            right = jnp.concatenate(
                [orbitals[ELEC * w + at : ELEC * w + at + HALF] for w in group]
                + [jnp.zeros((128 - rows, 128), F32)],
                axis=0,
            )
            left_high, left_low = split(left)
            right_high, right_low = split(right)
            product = dot(
                jnp.concatenate([left_high, left_low], axis=1),
                jnp.concatenate([right_high, right_high], axis=0),
            ) + dot(left_high, right_low)
            product = jnp.where((lanes >= at) & (lanes < at + HALF), product, 0.0)
            total = total + product * product
        for i in range(len(group)):
            totals.append(jnp.sum(total[HALF * i : HALF * i + HALF], axis=0, keepdims=True))
    total = jnp.sum(jnp.concatenate(totals, axis=0), axis=1, keepdims=True)
    out.append((jnp.log(total / (2.0 * HALF * HALF) + 1e-05), largest))


def interleaved(blocks):
    waiting, running = list(blocks), []
    while waiting or running:
        if waiting:
            running.append(waiting.pop(0))
        running = [block for block in running if next(block, 0) is None]


def pack_kernel(feats, inverses, w_embed, w_qkv, w_out, w_mlp, w_orb, packed, local):
    packed[:, 0:OUT_AT] = w_qkv[0, 0]
    packed[:, OUT_AT:MLP_AT] = w_out[0, 0]
    packed[:, MLP_AT:ORB_AT] = w_mlp[0, 0]
    packed[:, ORB_AT:EMB_AT] = jnp.concatenate(
        [w_orb[0], jnp.zeros((w_orb.shape[1], 128 - ELEC), F32)], axis=1
    )
    for j in range(4):
        packed[8 * j : 8 * j + 8, EMB_AT:PACKED] = w_embed[0, :, 128 * j : 128 * j + 128]
    local[0:8] = feats[0]
    for group in range(3):
        for spin in range(2):
            parts = [
                inverses[0, w, spin] if w < 8 else jnp.zeros((HALF, HALF), F32)
                for w in range(3 * group, 3 * group + 3)
            ]
            parts.append(jnp.zeros((HALF, 8), F32))
            local[8 + group, HALF * spin : HALF * spin + HALF, :] = jnp.concatenate(parts, axis=1)


def pack(*arrays):
    return pl.pallas_call(
        pack_kernel,
        out_shape=[
            jax.ShapeDtypeStruct((32, PACKED), F32),
            jax.ShapeDtypeStruct((11, ELEC, 128), F32),
        ],
        compiler_params=pltpu.CompilerParams(vmem_limit_bytes=58 * 2**20),
    )(*arrays)


def evaluate(jobs, weights, rows):
    outs = [[] for _ in jobs]

    def inverse_of(pack):
        return lambda group, spin: pack[8 + group, HALF * spin : HALF * spin + HALF, :]

    interleaved(
        walkers_block(
            pack[0:8].reshape(8 * ELEC, 128), inverse_of(pack), weights, precise, False, out
        )
        for (pack, _, precise), out in zip(jobs, outs)
    )
    lane = lax.broadcasted_iota(jnp.int32, (8, 128), 1)
    walker = lax.broadcasted_iota(jnp.int32, (8, 128), 0)
    for i, (pack, first, precise) in enumerate(jobs):
        results, largest = outs[i][0]
        rows[i : i + 1] = jnp.sum(
            jnp.where(lane == first + walker, results, 0.0), axis=0, keepdims=True
        )

        @pl.when(jnp.logical_not(jnp.max(largest) < SAFE))
        def _(i=i, pack=pack, first=first, precise=precise):
            rows[i : i + 1] = jnp.zeros((1, 128), F32)

            @pl.loop(0, 8)
            def _(w):
                turn = lax.rem(128 - HALF * lax.rem(w, 3), 128)
                group = w // 3

                def inverse(_, spin):
                    part = pack[8 + group, HALF * spin : HALF * spin + HALF, :]
                    return pltpu.roll(part, turn, 1)

                out = []
                interleaved([walkers_block(pack[w], inverse, weights, precise, True, out)])
                rows[i : i + 1] += jnp.where(lane[0:1] == first + w, out[0][0], 0.0)


def near_kernel(
    place, counts, local, group, packed, table, own, w_in, w_back, w_mlp, w_orb,
    in_all, back_all, mlp_all, orb_all, wide, rows, sems
):
    step = pl.program_id(0)
    state = place[0]
    low = lax.rem(state, 4)
    lane = lax.broadcasted_iota(jnp.int32, (1, 128), 1)

    def near(i):
        at = lax.rem(low + i, 4)
        return group.at[at], (state - low + at) * 8, False

    @pl.when(step == 0)
    def _():
        edges = [(ORB_AT, PACKED)] + [(at, at + 512) for at in range(0, ORB_AT, 512)]
        copies = []
        for i, (start, stop) in enumerate(edges):
            copies.append(
                pltpu.make_async_copy(
                    packed.at[:, start:stop], wide.at[:, start:stop], sems.at[i]
                )
            )
            copies[-1].start()
        prepare(wide, in_all, back_all, mlp_all, orb_all, copies)
        w_in[0] = in_all[0]
        w_back[0] = back_all[0]
        w_mlp[0] = mlp_all[0]
        w_orb[0] = orb_all[0]
        evaluate(
            [(local, state * 8, True), near(1)], (in_all, back_all, mlp_all, orb_all), rows
        )
        first = rows[0:1]
        turned = jnp.zeros((1, 128), F32)
        for s in range(8):
            mine = (lane < 8) & (state == s)
            turned = turned + jnp.where(mine, pltpu.roll(first, (128 - 8 * s) % 128, 1), 0.0)
        own[...] = turned
        table[...] = (
            first + rows[1:2] + jnp.where(lane == 64, counts[0].astype(F32), 0.0)
        )

    @pl.when(step > 0)
    def _():
        evaluate([near(2), near(3)], (in_all, back_all, mlp_all, orb_all), rows)
        table[...] += rows[0:1] + rows[1:2]


def far_kernel(place, start, group, w_in, w_back, w_mlp, w_orb, table, rows):
    step = pl.program_id(0)
    first = lax.rem(place[0] // 4 + 1, 2) * 4

    @pl.when(step == 0)
    def _():
        table[...] = jnp.broadcast_to(start[...], table.shape)

    evaluate(
        [(group.at[2 * step + i], (first + 2 * step + i) * 8, False) for i in range(2)],
        (w_in, w_back, w_mlp, w_orb),
        rows,
    )
    table[...] += jnp.broadcast_to(rows[0:1] + rows[1:2], table.shape)


def hold(*zeros):
    return lambda i, *scalars: zeros


def networks(place, counts, local, group, other, packed):
    weights = [(256, 1536), (1024, 512), (512, 512), (512, 128)]
    whole = [pl.BlockSpec((1,) + shape, hold(0, 0, 0)) for shape in weights]
    params = pltpu.CompilerParams(vmem_limit_bytes=50 * 2**20)
    rows = pltpu.VMEM((8, 128), F32)
    start, own, *prepared = pl.pallas_call(
        near_kernel,
        grid_spec=pltpu.PrefetchScalarGridSpec(
            num_scalar_prefetch=2,
            grid=(2,),
            in_specs=[
                pl.BlockSpec((11, ELEC, 128), hold(0, 0, 0)),
                pl.BlockSpec((4, 11, ELEC, 128), hold(0, 0, 0, 0)),
                pl.BlockSpec(memory_space=pl.ANY),
            ],
            out_specs=[pl.BlockSpec((1, 128), hold(0, 0)), pl.BlockSpec((1, 128), hold(0, 0))]
            + whole,
            scratch_shapes=[pltpu.VMEM((2,) + shape, BF) for shape in weights]
            + [pltpu.VMEM((512, PACKED), F32), rows, pltpu.SemaphoreType.DMA((6,))],
        ),
        out_shape=[jax.ShapeDtypeStruct((1, 128), F32)] * 2
        + [jax.ShapeDtypeStruct((1,) + shape, BF) for shape in weights],
        compiler_params=params,
        cost_estimate=pl.CostEstimate(
            flops=20_000_000_000, bytes_accessed=10_000_000, transcendentals=5_000_000
        ),
    )(place, counts, local, group, packed)
    table = pl.pallas_call(
        far_kernel,
        grid_spec=pltpu.PrefetchScalarGridSpec(
            num_scalar_prefetch=1,
            grid=(2,),
            in_specs=[
                pl.BlockSpec((1, 128), hold(0, 0)),
                pl.BlockSpec((4, 11, ELEC, 128), hold(0, 0, 0, 0)),
            ]
            + whole,
            out_specs=pl.BlockSpec((128, 128), hold(0, 0)),
            scratch_shapes=[rows],
        ),
        out_shape=jax.ShapeDtypeStruct((128, 128), F32),
        compiler_params=params,
        cost_estimate=pl.CostEstimate(
            flops=15_000_000_000, bytes_accessed=10_000_000, transcendentals=5_000_000
        ),
    )(place, start, other, *prepared)
    return table, own


def margin_kernel(place, received, margin, penalty):
    table = received[...]
    lane = lax.broadcasted_iota(jnp.int32, (16, 128), 1)
    block = lax.broadcasted_iota(jnp.int32, (16, 128), 0)
    owner = lane // 8
    own = jnp.zeros((16, 128), F32)
    counts = jnp.ones((1, 128), F32)
    for s in range(8):
        own = jnp.where(owner == s, table[16 * s : 16 * s + 16], own)
        counts = jnp.where(owner[0:1] == s, table[16 * s : 16 * s + 1, 64:65], counts)
    walker = (block * 8 + lane % 8).astype(F32)
    valid = (walker < counts) & (lane < 64)
    rows = []
    for t in range(8):
        ratio = jnp.exp(jnp.where(valid, table[16 * t : 16 * t + 16] - own, -jnp.inf))
        rows.append(jnp.sum(ratio, axis=0, keepdims=True))
    sums = jnp.concatenate(rows, axis=0) / counts
    pick = (
        lax.broadcasted_iota(jnp.int32, (8, 128), 1) // 8
        == lax.broadcasted_iota(jnp.int32, (8, 128), 0)
    ).astype(F32)

    def exact(left, right):
        return lax.dot_general(
            left,
            right,
            (((1,), (1,)), ((), ())),
            precision=lax.Precision.HIGHEST,
            preferred_element_type=F32,
        )

    by_state = exact(pick, sums)
    by_network = exact(sums, pick)
    row = lax.broadcasted_iota(jnp.int32, (8, 8), 0)
    column = lax.broadcasted_iota(jnp.int32, (8, 8), 1)
    margin[...] = jnp.sum(jnp.where(row == place[0], by_state, 0.0), axis=0, keepdims=True)
    product = jnp.where(column < row, by_state * by_network, 0.0)
    total = jnp.sum(jnp.sum(product, axis=0, keepdims=True), axis=1, keepdims=True)
    penalty[...] = 4.0 * total


def margins(place, received):
    return pl.pallas_call(
        margin_kernel,
        grid_spec=pltpu.PrefetchScalarGridSpec(
            num_scalar_prefetch=1,
            grid=(1,),
            in_specs=[pl.BlockSpec((128, 128), lambda i, place: (0, 0))],
            out_specs=[
                pl.BlockSpec((1, 8), lambda i, place: (0, 0)),
                pl.BlockSpec((1, 1), lambda i, place: (0, 0)),
            ],
        ),
        out_shape=[
            jax.ShapeDtypeStruct((1, 8), F32),
            jax.ShapeDtypeStruct((1, 1), F32),
        ],
        compiler_params=pltpu.CompilerParams(vmem_limit_bytes=4 * 2**20),
    )(place, received)


def on_device(feats, inverses, counts, w_embed, w_qkv, w_out, w_mlp, w_orb):
    me = lax.axis_index("state")
    packed, local = pack(feats, inverses, w_embed, w_qkv, w_out, w_mlp, w_orb)
    packed = lax.all_gather(packed, "walk", axis=0, tiled=True)
    partner = lax.ppermute(local, "state", [(i, i ^ 4) for i in range(8)])

    def along(block):
        wide = jnp.broadcast_to(block[None], (4,) + block.shape)
        return lax.all_to_all(
            wide, "state", 0, 0, axis_index_groups=[[0, 1, 2, 3], [4, 5, 6, 7]]
        )

    group = along(local)
    other = along(partner)
    place = me[None].astype(jnp.int32)
    table, own = networks(place, counts, local, group, other, packed)
    received = lax.all_to_all(
        table.reshape(128, 1, 128), ("state", "walk"), 0, 0, tiled=True
    )
    margin, penalty = margins(place, received.reshape(128, 128))
    return own[:, 0:8], margin, penalty[0, 0]


def solution(mesh):
    in_specs = (
        P("state", "walk", None, None),
        P("state", "walk", None, None, None),
        P("state"),
        P("state", "walk", None),
        P("state", None, "walk", None),
        P("state", None, "walk", None),
        P("state", None, "walk", None),
        P("state", "walk", None),
    )
    out_specs = (P("state", "walk"), P("state", None), P())
    return jax.shard_map(
        on_device, mesh=mesh, in_specs=in_specs, out_specs=out_specs, check_vma=False
    )
```

time: 151 us -> 128 us (0.85)
  Pallas kernels: 52.5 us -> 44 us
  local copies, waits for them, and re-layouts: 10.3 us -> 4.27 us
  waiting for transfers between devices: 39.5 us -> 34.1 us
  blocking collectives: 20.5 us -> 17 us
    all_to_all x2, waiting for transfers between devices: 21 us -> 3.11 us  [along(): lax.all_to_all(wide, 'state', 0, 0, axis_index_groups=[[0, 1, 2, 3], [4,...]
    all_gather x1, waiting for transfers between devices: 0.01 us -> 15.2 us  [on_device(): packed = lax.all_gather(packed, 'walk', axis=0, tiled=True)]
    pallas_call x1 -> x3, Pallas kernels: 50.1 us -> 43.2 us  [the longest x1 25.4 us: networks(): pl.pallas_call(near_kernel, grid_spec=pltpu.PrefetchScalarGridSpec(num_sc...]
    unnamed x15 -> x4, local copies, waits for them, and re-layouts: 4.84 us -> 0.44 us
    all_to_all x1, blocking collectives: 20.5 us -> 17 us  [on_device(): lax.all_to_all(table.reshape(128, 1, 128), ('state', 'walk'), 0, 0, tiled...]
    ppermute x1, waiting for transfers between devices: 18.5 us -> 15.8 us  [on_device(): partner = lax.ppermute(local, 'state', [(i, i ^ 4) for i in range(8)])]
    another operation x2 -> x0, local copies, waits for them, and re-layouts: 1.77 us -> none  [the longest x1 1.09 us: on_device(): flat = jnp.pad(inverses[0].reshape(8, ELEC, HALF), ((0, 1), (0, 0), (0, 0)))]
  transfers between devices with their start and end apart: 4 -> 4, of which waited for: 3 -> 3; matrix products, arithmetic and copies ran while one was open for 3% -> 3% of each run, Pallas kernels for 0% -> 20%
where the time goes in v2:
time: 128 us; the launch traced here: 127 us
  Pallas kernels  44 us (34%)
  waiting for transfers between devices  34.1 us (27%)
  blocking collectives  17 us (13%)
  between operations  14.7 us (11%)
  starting transfers between devices  13.2 us (10%)
  local copies, waits for them, and re-layouts  4.27 us (3%)
    pallas_call x1, Pallas kernels, networks(): pl.pallas_call(near_kernel, grid_spec=pltpu.PrefetchScalarGridSpec(num_sc...  25.4 us
    all_to_all x1, blocking collectives, on_device(): lax.all_to_all(table.reshape(128, 1, 128), ('state', 'walk'), 0, 0, tiled...  17 us
    ppermute x1, waiting for transfers between devices, on_device(): partner = lax.ppermute(local, 'state', [(i, i ^ 4) for i in range(8)])  15.8 us
    pallas_call x1, Pallas kernels, networks(): pl.pallas_call(far_kernel, grid_spec=pltpu.PrefetchScalarGridSpec(num_sca...  15.7 us
    all_gather x1, waiting for transfers between devices, on_device(): packed = lax.all_gather(packed, 'walk', axis=0, tiled=True)  15.2 us
    all_to_all x2, starting transfers between devices, along(): lax.all_to_all(wide, 'state', 0, 0, axis_index_groups=[[0, 1, 2, 3], [4,...  10.4 us
    broadcast_in_dim x2, local copies, waits for them, and re-layouts, along(): wide = jnp.broadcast_to(block[None], (4,) + block.shape)  3.83 us
    all_to_all x2, waiting for transfers between devices, along(): lax.all_to_all(wide, 'state', 0, 0, axis_index_groups=[[0, 1, 2, 3], [4,...  3.11 us
  transfers between devices with their start and end apart: 4, of which 3 were waited for; matrix products, arithmetic and copies ran while one was open for 3% of the time, Pallas kernels for 20%

profile of v2, /device:TPU:1, one launch (start us, length us, event | category | flops | bytes accessed | tf_op | source)
XLA Modules:
  0.0 127.2 jit_solution(7808791581053097531)
XLA Ops:
  7.2 0.0 all-gather.2.cloned.1.call-start
  7.2 2.1 %shard_map.103 = (f32[32,2816]{1,0:T(8,128)}, f32[11,80,128]{2,1,0:T(8,128)}) custom-call(f32[1,8,80,128]{3,2,1,0:T(8,128)} %feats.1, f32[1,8,2,40,40]{4,3,2,1,0:T(8,128)} %inverses.1, f32[1,8,512]{2,1,0:T(8,128)} %w_embed.1, f32[1,1,32,1536]{3,2,1,0:T(8,128)} %w_qkv.1, f32[1,1,32,512]{3,2,1,0:T(8,128)} %w_out.1, f32[1,1,32,512]{3,2,1,0:T(8,128)} %w_mlp.1, ...), custom_call_target="tpu_custom_call" | custom-call | tf_op jit(solution)/shard_map/pallas_call | solution.py:260
  9.3 0.0 all-gather.2.cloned.1.call-update
  9.4 2.4 %broadcast_in_dim.7 = f32[4,11,80,128]{3,2,1,0:T(8,128)} broadcast(f32[11,80,128]{2,1,0:T(8,128)} %get-tuple-element.13.local), dimensions={1,2,3} | broadcast | bytes 2252800 | tf_op jit(solution)/shard_map/broadcast_in_dim | solution.py:493
  11.7 0.0 copy-start
  11.7 6.0 %all-to-all-start = ((f32[4,11,80,128]{3,2,1,0:T(8,128)}), f32[4,11,80,128]{3,2,1,0:T(8,128)S(1)}, u32[]{:S(2)}, u32[]{:S(2)}) async-start(f32[4,11,80,128]{3,2,1,0:T(8,128)} %broadcast_in_dim.7), calls=%async_computation | async-start | bytes 3604480 | tf_op jit(solution)/shard_map/all_to_all | solution.py:494
  17.7 0.0 copy-done
  17.7 2.7 %collective-permute-start = (f32[11,80,128]{2,1,0:T(8,128)S(1)}, f32[11,80,128]{2,1,0:T(8,128)S(1)}, u32[]{:S(2)}, u32[]{:S(2)}) collective-permute-start(f32[11,80,128]{2,1,0:T(8,128)S(1)} %copy-done), channel_id=1, source_target_pairs={{0,64},{16,80},{32,96},{48,112},{64,0},{80,16},{96,32},{112,48},{1... | collective-permute-start | bytes 1351688 | tf_op jit(solution)/shard_map/ppermute | solution.py:490
  21.1 15.8 %collective-permute-done = f32[11,80,128]{2,1,0:T(8,128)S(1)} collective-permute-done((f32[11,80,128]{2,1,0:T(8,128)S(1)}, f32[11,80,128]{2,1,0:T(8,128)S(1)}, u32[]{:S(2)}, u32[]{:S(2)}) %collective-permute-start) | collective-permute-done | bytes 450592 | tf_op jit(solution)/shard_map/ppermute | solution.py:490
  36.9 3.1 %all-to-all-done.group = f32[4,11,80,128]{3,2,1,0:T(8,128)S(1)} async-done(((f32[4,11,80,128]{3,2,1,0:T(8,128)}), f32[4,11,80,128]{3,2,1,0:T(8,128)S(1)}, u32[]{:S(2)}, u32[]{:S(2)}) %all-to-all-start) | async-done | bytes 1802272 | tf_op jit(solution)/shard_map/all_to_all | solution.py:494
  40.0 0.0 copy-start.1
  40.0 1.5 %broadcast_in_dim.8 = f32[4,11,80,128]{3,2,1,0:T(8,128)} broadcast(f32[11,80,128]{2,1,0:T(8,128)S(1)} %collective-permute-done), dimensions={1,2,3} | broadcast | bytes 2252800 | tf_op jit(solution)/shard_map/broadcast_in_dim | solution.py:493
  41.5 0.4 copy-done.1
  41.9 4.4 %all-to-all-start.1 = ((f32[4,11,80,128]{3,2,1,0:T(8,128)}), f32[4,11,80,128]{3,2,1,0:T(8,128)}, u32[]{:S(2)}, u32[]{:S(2)}) async-start(f32[4,11,80,128]{3,2,1,0:T(8,128)} %broadcast_in_dim.8), calls=%async_computation.1 | async-start | bytes 3604480 | tf_op jit(solution)/shard_map/all_to_all | solution.py:494
  46.3 15.2 %all-gather.2.cloned.1.call-done.packed = f32[512,2816]{1,0:T(8,128)} async-done(((f32[32,2816]{1,0:T(8,128)}), f32[512,2816]{1,0:T(8,128)}) %all-gather.2.cloned.1.call-update) | async-done | bytes 5767184 | tf_op jit(solution)/shard_map/all_gather | solution.py:489
  61.5 25.4 %shard_map.104 = (f32[1,128]{1,0:T(1,128)S(1)}, f32[1,128]{1,0:T(1,128)}, bf16[1,256,1536]{2,1,0:T(8,128)(2,1)S(1)}, bf16[1,1024,512]{2,1,0:T(8,128)(2,1)S(1)}, ...) custom-call(s32[1]{0:T(128)} %bitcast.place, s32[1]{0:T(128)S(6)} %copy.12.counts, ...), custom_call_target="tpu_custom_call" | custom-call | flops 20000000000 | bytes 10000000 | tf_op jit(solution)/shard_map/pallas_call | solution.py:381
  86.9 0.0 all-to-all-done.1.group
  86.9 15.7 %shard_map.105 = f32[128,128]{1,0:T(8,128)S(1)} custom-call(s32[1]{0:T(128)} %bitcast.place, f32[1,128]{1,0:T(1,128)S(1)} %get-tuple-element.16.start, f32[4,11,80,128]{3,2,1,0:T(8,128)} %all-to-all-done.1.group, bf16[1,256,1536]{2,1,0:T(8,128)(2,1)S(1)} %get-tuple-element.17.w_in, bf16[1,1024,512]{2,1,0:T(8,128)(2,1)S(1)} %get-tuple-element.18.w_back, ...), custom_call_target="tpu_custom_call" | custom-call | flops 15000000512 | bytes 10000000 | tf_op jit(solution)/shard_map/pallas_call | solution.py:403
  102.6 17.0 %all_to_all.15 = f32[128,1,128]{2,1,0:T(1,128)S(1)} all-to-all(f32[128,1,128]{2,1,0:T(1,128)S(1)} %bitcast.8), channel_id=1, replica_groups=mesh['state'=8,'walk'=16] {'state','walk'}, dimensions={0} | all-to-all | bytes 131072 | tf_op jit(solution)/shard_map/all_to_all | solution.py:502
  119.5 0.8 shard_map.106
Async XLA Ops:
  7.2 54.4 %all-gather.2.cloned.1.call-start = ((), (), s32[]{:S(2)}) async-start(), calls=%async_computation.3 | async-start | bytes 6127616 | tf_op jit(solution)/shard_map/all_gather | solution.py:489
  11.7 6.0 %copy-start = (f32[11,80,128]{2,1,0:T(8,128)S(1)}, f32[11,80,128]{2,1,0:T(8,128)}, u32[]{:S(2)}) copy-start(f32[11,80,128]{2,1,0:T(8,128)} %get-tuple-element.13.local) | copy-start | bytes 1351684
  11.7 28.2 %all-to-all-start = ((f32[4,11,80,128]{3,2,1,0:T(8,128)}), f32[4,11,80,128]{3,2,1,0:T(8,128)S(1)}, u32[]{:S(2)}, u32[]{:S(2)}) async-start(f32[4,11,80,128]{3,2,1,0:T(8,128)} %broadcast_in_dim.7), calls=%async_computation | async-start | bytes 3604480 | tf_op jit(solution)/shard_map/all_to_all | solution.py:494
  17.7 19.2 %collective-permute-start = (f32[11,80,128]{2,1,0:T(8,128)S(1)}, f32[11,80,128]{2,1,0:T(8,128)S(1)}, u32[]{:S(2)}, u32[]{:S(2)}) collective-permute-start(f32[11,80,128]{2,1,0:T(8,128)S(1)} %copy-done), channel_id=1, source_target_pairs={{0,64},{16,80},{32,96},{48,112},{64,0},{80,16},{96,32},{112,48},{1... | collective-permute-start | bytes 1351688 | tf_op jit(solution)/shard_map/ppermute | solution.py:490
  40.0 1.9 %copy-start.1 = (f32[4,11,80,128]{3,2,1,0:T(8,128)}, f32[4,11,80,128]{3,2,1,0:T(8,128)S(1)}, u32[]{:S(2)}) copy-start(f32[4,11,80,128]{3,2,1,0:T(8,128)S(1)} %all-to-all-done.group) | copy-start | bytes 5406724
  41.9 45.0 %all-to-all-start.1 = ((f32[4,11,80,128]{3,2,1,0:T(8,128)}), f32[4,11,80,128]{3,2,1,0:T(8,128)}, u32[]{:S(2)}, u32[]{:S(2)}) async-start(f32[4,11,80,128]{3,2,1,0:T(8,128)} %broadcast_in_dim.8), calls=%async_computation.1 | async-start | bytes 3604480 | tf_op jit(solution)/shard_map/all_to_all | solution.py:494
Sparse Core Ops, SparseCore 0:
  9.7 51.7 all-gather.1

commit v3 on v2

--- a/solution.py
+++ b/solution.py
@@ -48,11 +48,18 @@
 
 
 def prepare(packed, w_in, w_back, w_mlp, w_orb, copies):
-    shards = packed.shape[0] // 32
+    def fold(left, right):
+        left_high, left_low = split(left)
+        right_high, right_low = split(right)
+        both = dot(jnp.concatenate([left_high, left_low], axis=0), right_high)
+        return both[:128] + both[128:] + dot(left_high, right_low)
+
     copies[0].wait()
     parts = []
     for j in range(4):
-        rows = [packed[i * 32 + 8 * j : i * 32 + 8 * j + 8, EMB_AT:PACKED] for i in range(shards)]
+        rows = [
+            packed[i * 32 + 8 * j : i * 32 + 8 * j + 8, EMB_AT:PACKED] for i in range(16)
+        ]
         parts.append(jnp.concatenate(rows, axis=0))
     embed = jnp.concatenate(parts, axis=1)
     centred = embed - jnp.mean(embed, axis=1, keepdims=True)
@@ -66,21 +73,28 @@
 
     put(0, embed)
     copies[1].wait()
-    query = dot3(centred, packed[:, 0:512], dot) * (math.log2(math.e) / 8.0)
+    query = fold(centred, packed[:, 0:512]) * (math.log2(math.e) / 8.0)
     copies[2].wait()
-    keys = dot3(centred, packed[:, 512:1024], dot)
+    keys = fold(centred, packed[:, 512:1024])
     copies[3].wait()
-    values = dot3(centred, packed[:, 1024:1536], dot)
+    values = fold(centred, packed[:, 1024:1536])
+    copies[4].wait()
     lane = lax.broadcasted_iota(jnp.int32, (128, 128), 1)
-    copies[4].wait()
-    for head in range(8):
-        pair = slice(128 * (head // 2), 128 * (head // 2) + 128)
-        keep = (lane < 64) if head % 2 == 0 else (lane >= 64)
-        put(512 + 128 * head, dot3(jnp.where(keep, query[:, pair], 0.0), keys[:, pair], dot_nt))
-        back = dot3(jnp.where(keep, values[:, pair], 0.0), packed[pair, OUT_AT:MLP_AT], dot)
-        high, low = split(back)
-        w_back[0, 128 * head : 128 * head + 128, :] = high
-        w_back[1, 128 * head : 128 * head + 128, :] = low
+
+    def heads(matrix):
+        return jnp.concatenate(
+            [jnp.where(lane < 64, matrix, 0.0), jnp.where(lane >= 64, matrix, 0.0)], axis=0
+        )
+
+    for pair in range(4):
+        at = slice(128 * pair, 128 * pair + 128)
+        both = dot3(heads(query[:, at]), keys[:, at], dot_nt)
+        put(512 + 256 * pair, both[:128])
+        put(640 + 256 * pair, both[128:])
+        both = dot3(heads(values[:, at]), packed[at, OUT_AT:MLP_AT], dot)
+        high, low = split(both)
+        w_back[0, 256 * pair : 256 * pair + 256, :] = high
+        w_back[1, 256 * pair : 256 * pair + 256, :] = low
     copies[5].wait()
     for ref, at, width in ((w_mlp, MLP_AT, 512), (w_orb, ORB_AT, 128)):
         high, low = split(packed[:, at : at + width])
@@ -162,7 +176,10 @@
         right = jnp.concatenate([padded(high, w), live], axis=1)
         if precise:
             weights_high, weights_low = weights[w]
-            both = dot(weights_high, right) + dot(weights_low, right)
+            both = dot(
+                jnp.concatenate([weights_high, weights_low], axis=1),
+                jnp.concatenate([right, right], axis=0),
+            )
             sums.append((both[:, :128] + dot(weights_high, padded(low, w)), both[:, 128:]))
         else:
             both = dot(weights[w], right)
@@ -236,7 +253,7 @@
         running = [block for block in running if next(block, 0) is None]
 
 
-def pack_kernel(feats, inverses, w_embed, w_qkv, w_out, w_mlp, w_orb, packed, local):
+def pack_weights_kernel(w_embed, w_qkv, w_out, w_mlp, w_orb, packed):
     packed[:, 0:OUT_AT] = w_qkv[0, 0]
     packed[:, OUT_AT:MLP_AT] = w_out[0, 0]
     packed[:, MLP_AT:ORB_AT] = w_mlp[0, 0]
@@ -245,6 +262,9 @@
     )
     for j in range(4):
         packed[8 * j : 8 * j + 8, EMB_AT:PACKED] = w_embed[0, :, 128 * j : 128 * j + 128]
+
+
+def pack_walkers_kernel(feats, inverses, local, wide):
     local[0:8] = feats[0]
     for group in range(3):
         for spin in range(2):
@@ -254,15 +274,14 @@
             ]
             parts.append(jnp.zeros((HALF, 8), F32))
             local[8 + group, HALF * spin : HALF * spin + HALF, :] = jnp.concatenate(parts, axis=1)
-
-
-def pack(*arrays):
+    for to in range(4):
+        wide[to] = local[...]
+
+
+def pack(kernel, shapes, *arrays):
     return pl.pallas_call(
-        pack_kernel,
-        out_shape=[
-            jax.ShapeDtypeStruct((32, PACKED), F32),
-            jax.ShapeDtypeStruct((11, ELEC, 128), F32),
-        ],
+        kernel,
+        out_shape=[jax.ShapeDtypeStruct(shape, F32) for shape in shapes],
         compiler_params=pltpu.CompilerParams(vmem_limit_bytes=58 * 2**20),
     )(*arrays)
 
@@ -485,18 +504,18 @@
 
 def on_device(feats, inverses, counts, w_embed, w_qkv, w_out, w_mlp, w_orb):
     me = lax.axis_index("state")
-    packed, local = pack(feats, inverses, w_embed, w_qkv, w_out, w_mlp, w_orb)
+    (packed,) = pack(
+        pack_weights_kernel, [(32, PACKED)], w_embed, w_qkv, w_out, w_mlp, w_orb
+    )
     packed = lax.all_gather(packed, "walk", axis=0, tiled=True)
+    local, wide = pack(
+        pack_walkers_kernel, [(11, ELEC, 128), (4, 11, ELEC, 128)], feats, inverses
+    )
+    along = [[0, 1, 2, 3], [4, 5, 6, 7]]
+    group = lax.all_to_all(wide, "state", 0, 0, axis_index_groups=along)
     partner = lax.ppermute(local, "state", [(i, i ^ 4) for i in range(8)])
-
-    def along(block):
-        wide = jnp.broadcast_to(block[None], (4,) + block.shape)
-        return lax.all_to_all(
-            wide, "state", 0, 0, axis_index_groups=[[0, 1, 2, 3], [4, 5, 6, 7]]
-        )
-
-    group = along(local)
-    other = along(partner)
+    wide = jnp.broadcast_to(partner[None], (4,) + partner.shape)
+    other = lax.all_to_all(wide, "state", 0, 0, axis_index_groups=along)
     place = me[None].astype(jnp.int32)
     table, own = networks(place, counts, local, group, other, packed)
     received = lax.all_to_all(

time: 128 us -> 127 us (level)
  local copies, waits for them, and re-layouts: 4.27 us -> 1.9 us
  Pallas kernels: 44 us -> 45.5 us
    broadcast_in_dim x2 -> x1, local copies, waits for them, and re-layouts: 3.83 us -> 1.46 us  [on_device(): wide = jnp.broadcast_to(partner[None], (4,) + partner.shape)]
    pallas_call x1 -> x2, Pallas kernels: 2.13 us -> 4.35 us  [pack(): pl.pallas_call(kernel, out_shape=[jax.ShapeDtypeStruct(shape, F32) for sh...]
  transfers between devices with their start and end apart: 4 -> 4, of which waited for: 3 -> 3; matrix products, arithmetic and copies ran while one was open for 3% -> 1% of each run, Pallas kernels for 20% -> 22%
where the time goes in v3:
time: 127 us; the launch traced here: 126 us
  Pallas kernels  45.5 us (36%)
  waiting for transfers between devices  33.9 us (27%)
  blocking collectives  17.2 us (14%)
  between operations  14.7 us (12%)
  starting transfers between devices  13.2 us (10%)
  local copies, waits for them, and re-layouts  1.9 us (1%)
    pallas_call x1, Pallas kernels, networks(): pl.pallas_call(near_kernel, grid_spec=pltpu.PrefetchScalarGridSpec(num_sc...  24.7 us
    all_to_all x1, blocking collectives, on_device(): lax.all_to_all(table.reshape(128, 1, 128), ('state', 'walk'), 0, 0, tiled...  17.2 us
    pallas_call x1, Pallas kernels, networks(): pl.pallas_call(far_kernel, grid_spec=pltpu.PrefetchScalarGridSpec(num_sca...  15.6 us
    ppermute x1, waiting for transfers between devices, on_device(): partner = lax.ppermute(local, 'state', [(i, i ^ 4) for i in range(8)])  15.2 us
    all_gather x1, waiting for transfers between devices, on_device(): packed = lax.all_gather(packed, 'walk', axis=0, tiled=True)  15 us
    all_to_all x1, starting transfers between devices, on_device(): group = lax.all_to_all(wide, 'state', 0, 0, axis_index_groups=along)  5.99 us
    all_to_all x1, starting transfers between devices, on_device(): other = lax.all_to_all(wide, 'state', 0, 0, axis_index_groups=along)  4.39 us
    pallas_call x2, Pallas kernels, pack(): pl.pallas_call(kernel, out_shape=[jax.ShapeDtypeStruct(shape, F32) for sh...  4.35 us
  transfers between devices with their start and end apart: 4, of which 3 were waited for; matrix products, arithmetic and copies ran while one was open for 1% of the time, Pallas kernels for 22%

profile of v3, /device:TPU:1, one launch (start us, length us, event | category | flops | bytes accessed | tf_op | source)
XLA Modules:
  0.0 126.4 jit_solution(3408979288334268170)
XLA Ops:
  7.2 0.0 all-gather.2.cloned.1.call-start
  7.2 1.7 %shard_map.104 = f32[32,2816]{1,0:T(8,128)} custom-call(f32[1,8,512]{2,1,0:T(8,128)} %w_embed.1, f32[1,1,32,1536]{3,2,1,0:T(8,128)} %w_qkv.1, f32[1,1,32,512]{3,2,1,0:T(8,128)} %w_out.1, f32[1,1,32,512]{3,2,1,0:T(8,128)} %w_mlp.1, f32[1,32,80]{2,1,0:T(8,128)} %w_orb.1), custom_call_target="tpu_custom_call" | custom-call | tf_op jit(solution)/shard_map/pallas_call | solution.py:282
  8.9 0.0 all-gather.2.cloned.1.call-update
  9.0 2.6 %shard_map.103 = (f32[11,80,128]{2,1,0:T(8,128)}, f32[4,11,80,128]{3,2,1,0:T(8,128)}) custom-call(f32[1,8,80,128]{3,2,1,0:T(8,128)} %feats.1, f32[1,8,2,40,40]{4,3,2,1,0:T(8,128)} %inverses.1), custom_call_target="tpu_custom_call" | custom-call | tf_op jit(solution)/shard_map/pallas_call | solution.py:282
  11.6 0.0 copy-start
  11.6 6.0 %all-to-all-start = ((f32[4,11,80,128]{3,2,1,0:T(8,128)}), f32[4,11,80,128]{3,2,1,0:T(8,128)S(1)}, u32[]{:S(2)}, u32[]{:S(2)}) async-start(f32[4,11,80,128]{3,2,1,0:T(8,128)} %get-tuple-element.14), calls=%async_computation | async-start | bytes 3604480 | tf_op jit(solution)/shard_map/all_to_all | solution.py:515
  17.6 0.0 copy-done
  17.6 2.7 %collective-permute-start = (f32[11,80,128]{2,1,0:T(8,128)S(1)}, f32[11,80,128]{2,1,0:T(8,128)S(1)}, u32[]{:S(2)}, u32[]{:S(2)}) collective-permute-start(f32[11,80,128]{2,1,0:T(8,128)S(1)} %copy-done), channel_id=1, source_target_pairs={{0,64},{16,80},{32,96},{48,112},{64,0},{80,16},{96,32},{112,48},{1... | collective-permute-start | bytes 1351688 | tf_op jit(solution)/shard_map/ppermute | solution.py:516
  21.0 15.2 %collective-permute-done = f32[11,80,128]{2,1,0:T(8,128)S(1)} collective-permute-done((f32[11,80,128]{2,1,0:T(8,128)S(1)}, f32[11,80,128]{2,1,0:T(8,128)S(1)}, u32[]{:S(2)}, u32[]{:S(2)}) %collective-permute-start) | collective-permute-done | bytes 450592 | tf_op jit(solution)/shard_map/ppermute | solution.py:516
  36.2 3.6 %all-to-all-done.group = f32[4,11,80,128]{3,2,1,0:T(8,128)S(1)} async-done(((f32[4,11,80,128]{3,2,1,0:T(8,128)}), f32[4,11,80,128]{3,2,1,0:T(8,128)S(1)}, u32[]{:S(2)}, u32[]{:S(2)}) %all-to-all-start) | async-done | bytes 1802272 | tf_op jit(solution)/shard_map/all_to_all | solution.py:515
  39.8 0.0 copy-start.1
  39.8 1.5 %broadcast_in_dim.10 = f32[4,11,80,128]{3,2,1,0:T(8,128)} broadcast(f32[11,80,128]{2,1,0:T(8,128)S(1)} %collective-permute-done), dimensions={1,2,3} | broadcast | bytes 2252800 | tf_op jit(solution)/shard_map/broadcast_in_dim | solution.py:517
  41.3 0.4 copy-done.1
  41.7 4.4 %all-to-all-start.1 = ((f32[4,11,80,128]{3,2,1,0:T(8,128)}), f32[4,11,80,128]{3,2,1,0:T(8,128)}, u32[]{:S(2)}, u32[]{:S(2)}) async-start(f32[4,11,80,128]{3,2,1,0:T(8,128)} %broadcast_in_dim.10), calls=%async_computation.1 | async-start | bytes 3604480 | tf_op jit(solution)/shard_map/all_to_all | solution.py:518
  46.1 15.0 %all-gather.2.cloned.1.call-done.packed = f32[512,2816]{1,0:T(8,128)} async-done(((f32[32,2816]{1,0:T(8,128)}), f32[512,2816]{1,0:T(8,128)}) %all-gather.2.cloned.1.call-update) | async-done | bytes 5767184 | tf_op jit(solution)/shard_map/all_gather | solution.py:510
  61.1 24.7 %shard_map.105 = (f32[1,128]{1,0:T(1,128)S(1)}, f32[1,128]{1,0:T(1,128)}, bf16[1,256,1536]{2,1,0:T(8,128)(2,1)S(1)}, bf16[1,1024,512]{2,1,0:T(8,128)(2,1)S(1)}, ...) custom-call(s32[1]{0:T(128)} %bitcast.place, s32[1]{0:T(128)S(6)} %copy.12.counts, ...), custom_call_target="tpu_custom_call" | custom-call | flops 20000000000 | bytes 10000000 | tf_op jit(solution)/shard_map/pallas_call | solution.py:400
  85.8 0.0 all-to-all-done.1.group
  85.8 15.6 %shard_map.106 = f32[128,128]{1,0:T(8,128)S(1)} custom-call(s32[1]{0:T(128)} %bitcast.place, f32[1,128]{1,0:T(1,128)S(1)} %get-tuple-element.16.start, f32[4,11,80,128]{3,2,1,0:T(8,128)} %all-to-all-done.1.group, bf16[1,256,1536]{2,1,0:T(8,128)(2,1)S(1)} %get-tuple-element.17.w_in, bf16[1,1024,512]{2,1,0:T(8,128)(2,1)S(1)} %get-tuple-element.18.w_back, ...), custom_call_target="tpu_custom_call" | custom-call | flops 15000000512 | bytes 10000000 | tf_op jit(solution)/shard_map/pallas_call | solution.py:422
  101.5 17.2 %all_to_all.15 = f32[128,1,128]{2,1,0:T(1,128)S(1)} all-to-all(f32[128,1,128]{2,1,0:T(1,128)S(1)} %bitcast.8), channel_id=1, replica_groups=mesh['state'=8,'walk'=16] {'state','walk'}, dimensions={0} | all-to-all | bytes 131072 | tf_op jit(solution)/shard_map/all_to_all | solution.py:521
  118.7 0.8 shard_map.107
Async XLA Ops:
  7.2 54.0 %all-gather.2.cloned.1.call-start = ((), (), s32[]{:S(2)}) async-start(), calls=%async_computation.3 | async-start | bytes 6127616 | tf_op jit(solution)/shard_map/all_gather | solution.py:510
  11.6 6.0 %copy-start = (f32[11,80,128]{2,1,0:T(8,128)S(1)}, f32[11,80,128]{2,1,0:T(8,128)}, u32[]{:S(2)}) copy-start(f32[11,80,128]{2,1,0:T(8,128)} %get-tuple-element.13.local) | copy-start | bytes 1351684
  11.6 28.2 %all-to-all-start = ((f32[4,11,80,128]{3,2,1,0:T(8,128)}), f32[4,11,80,128]{3,2,1,0:T(8,128)S(1)}, u32[]{:S(2)}, u32[]{:S(2)}) async-start(f32[4,11,80,128]{3,2,1,0:T(8,128)} %get-tuple-element.14), calls=%async_computation | async-start | bytes 3604480 | tf_op jit(solution)/shard_map/all_to_all | solution.py:515
  17.6 18.6 %collective-permute-start = (f32[11,80,128]{2,1,0:T(8,128)S(1)}, f32[11,80,128]{2,1,0:T(8,128)S(1)}, u32[]{:S(2)}, u32[]{:S(2)}) collective-permute-start(f32[11,80,128]{2,1,0:T(8,128)S(1)} %copy-done), channel_id=1, source_target_pairs={{0,64},{16,80},{32,96},{48,112},{64,0},{80,16},{96,32},{112,48},{1... | collective-permute-start | bytes 1351688 | tf_op jit(solution)/shard_map/ppermute | solution.py:516
  39.8 1.9 %copy-start.1 = (f32[4,11,80,128]{3,2,1,0:T(8,128)}, f32[4,11,80,128]{3,2,1,0:T(8,128)S(1)}, u32[]{:S(2)}) copy-start(f32[4,11,80,128]{3,2,1,0:T(8,128)S(1)} %all-to-all-done.group) | copy-start | bytes 5406724
  41.7 44.1 %all-to-all-start.1 = ((f32[4,11,80,128]{3,2,1,0:T(8,128)}), f32[4,11,80,128]{3,2,1,0:T(8,128)}, u32[]{:S(2)}, u32[]{:S(2)}) async-start(f32[4,11,80,128]{3,2,1,0:T(8,128)} %broadcast_in_dim.10), calls=%async_computation.1 | async-start | bytes 3604480 | tf_op jit(solution)/shard_map/all_to_all | solution.py:518
Sparse Core Ops, SparseCore 0:
  9.7 51.3 all-gather.1
